TPU v7x, 32 devices: a whole 2x2x4 slice. The times are simulated.
32 devices in a mesh: rep: 2 (over x), grp: 8 (over z, y), head: 2 (over core).
Axes of the slice: x: 2, y: 2, z: 4, core: 2. Of those that a mesh axis runs over, the one named last changes fastest.
Arguments:
- queries: bfloat16 [2048, 2560], P(('rep', 'grp'), 'head'), parts along dimension 0, may hold values from -180 to 180
- key_matrix: bfloat16 [2048, 512], P(('rep', 'grp'), 'head'), parts along dimension 0, may hold values from -5 to 5
- value_matrix: bfloat16 [2048, 512], P(('rep', 'grp'), 'head'), parts along dimension 0, may hold values from -5 to 5
- residual: bfloat16 [2048, 2560], P(('rep', 'grp', 'head')), parts along dimension 0, may hold values from -10 to 10
- norm_gain: bfloat16 [2560], replicated, may hold values from 0.099609375 to 1.8984375
- w_gate: bfloat16 [8, 2560, 4096], P('grp', None, 'head'), may hold values from -0.125 to 0.125
- w_up: bfloat16 [8, 2560, 4096], P('grp', None, 'head'), may hold values from -0.125 to 0.125
- w_down: bfloat16 [8, 4096, 2560], P('grp', 'head'), may hold values from -0.0625 to 0.0625
- owner_class: int32 [8], replicated, may hold values from 0 to 3, as said below
- class_counts: int32 [32, 4], P(('rep', 'grp', 'head')), parts along dimension 0, may hold values from 0 to 24, as said below
- episode_index: int32 [2048], P(('rep', 'grp')), parts along dimension 0, may hold values from 0 to 1022, as said below
Outputs:
- layer_out: bfloat16 [2048, 2560], P(('rep', 'grp', 'head')), parts along dimension 0
There are 2 independent parts, one for each index of `rep`. A program takes and returns all parts, laid end to end along the dimension named above; an argument that names none is the same for every part. Nothing has to cross between parts.
Inputs may be any that keep to these rules, and one draw needn't show every extreme that they name: `owner_class`: each class is owned by exactly 2 groups. `class_counts`: each row sums to 64; every count is even; in each draw one class has exactly 24 tokens on every device. `episode_index`: an episode's id is the index of its first token; ids never fall along the tokens; an episode begins at an even row and never spans two class runs or two shards of 64 rows.
All inputs are finite; a program needn't handle non-finite values.
Results may differ from a plain program's by a relative error of at most 0.0067.
Values may be sent and summed in bfloat16 or wider, within the bound.
A program may use at most 128 MiB of HBM per device.

v0:
```python
import math

import jax
import jax.numpy as jnp
from jax import lax
from jax.sharding import PartitionSpec as P

HEAD_SIZE = 128


def attend(queries, key_matrix, value_matrix, episode_index):
    length = queries.shape[0]
    kv_count = key_matrix.shape[1] // HEAD_SIZE
    head_repeats = queries.shape[1] // key_matrix.shape[1]
    query_tiles = queries.reshape(length, kv_count, head_repeats, HEAD_SIZE)
    key_tiles = key_matrix.reshape(length, kv_count, HEAD_SIZE)
    value_tiles = value_matrix.reshape(length, kv_count, HEAD_SIZE)
    logit_table = jnp.einsum(
        "envh,ynh->nvey", query_tiles, key_tiles, preferred_element_type=jnp.float32
    )
    logit_table = logit_table * (1.0 / math.sqrt(HEAD_SIZE))
    places = jnp.arange(length)
    allowed = (episode_index[:, None] == episode_index[None, :]) & (
        places[None, :] <= places[:, None]
    )
    logit_table = jnp.where(allowed, logit_table, -jnp.inf)
    softmax_probs = jax.nn.softmax(logit_table, axis=-1).astype(jnp.bfloat16)
    mixed_values = jnp.einsum(
        "alwn,nam->walm", softmax_probs, value_tiles, preferred_element_type=jnp.float32
    )
    return mixed_values.reshape(length, kv_count * head_repeats * HEAD_SIZE).astype(jnp.bfloat16)


def normalize(mixed_values, norm_gain):
    square = jnp.mean(mixed_values * mixed_values, axis=-1, keepdims=True)
    return (mixed_values * lax.rsqrt(square + 1e-06) * norm_gain.astype(jnp.float32)).astype(
        jnp.bfloat16
    )


def class_network(token_block, w_gate, w_up, w_down):
    sources, depth_rows, model_width = token_block.shape
    flattened = token_block.reshape(sources * depth_rows, model_width)
    gate_act = jnp.dot(flattened, w_gate[0], preferred_element_type=jnp.float32)
    up_act = jnp.dot(flattened, w_up[0], preferred_element_type=jnp.float32)
    hidden = (jax.nn.silu(gate_act) * up_act).astype(jnp.bfloat16)
    partial_out = jnp.dot(hidden, w_down[0], preferred_element_type=jnp.float32).astype(
        jnp.bfloat16
    )
    return partial_out.reshape(sources, depth_rows, model_width)


def answer_back(token_block, w_gate, w_up, w_down):
    partial_out = class_network(token_block, w_gate, w_up, w_down)
    return lax.all_to_all(partial_out, ("grp", "head"), split_axis=0, concat_axis=0, tiled=True)


def on_device(
    queries,
    key_matrix,
    value_matrix,
    residual,
    norm_gain,
    w_gate,
    w_up,
    w_down,
    owner_class,
    class_counts,
    episode_index,
):
    local_heads = attend(queries, key_matrix, value_matrix, episode_index)
    attention_output = lax.all_to_all(local_heads, "head", split_axis=0, concat_axis=1, tiled=True)
    mixed_values = residual.astype(jnp.float32) + attention_output.astype(jnp.float32)
    normed = normalize(mixed_values, norm_gain)
    shard_rows = residual.shape[0]
    model_width = residual.shape[1]
    capacity = 3 * shard_rows // 8
    class_total = class_counts.shape[1]
    group_count = owner_class.shape[0]
    core_total = lax.axis_size("head")
    counts = class_counts[0]
    run_ends = jnp.cumsum(counts)
    starts = run_ends - counts
    class_range = jnp.arange(class_total)
    owner_table = (owner_class[:, None] == class_range[None, :]).astype(jnp.int32)
    dest_start = jnp.sum(owner_table * starts[None, :], axis=1)
    dest_count = jnp.sum(owner_table * counts[None, :], axis=1)
    depth_range = jnp.arange(capacity)
    picked_index = jnp.clip(dest_start[:, None] + depth_range[None, :], 0, shard_rows - 1)
    filled = depth_range[None, :] < dest_count[:, None]
    outgoing = jnp.take(normed, picked_index.reshape(-1), axis=0).reshape(
        group_count, capacity, model_width
    )
    outgoing = jnp.where(filled[:, :, None], outgoing, jnp.zeros((), jnp.bfloat16))
    doubled = jnp.broadcast_to(outgoing[:, None], (group_count, core_total, capacity, model_width))
    doubled = doubled.reshape(group_count * core_total, capacity, model_width)
    returned = answer_back(
        lax.all_to_all(doubled, ("grp", "head"), split_axis=0, concat_axis=0, tiled=True),
        w_gate,
        w_up,
        w_down,
    )
    pair_sum = jnp.sum(
        returned.reshape(group_count, core_total, capacity, model_width).astype(jnp.float32), axis=1
    )
    returned = pair_sum.astype(jnp.bfloat16)
    owner_weights = owner_table.astype(jnp.bfloat16)
    class_sums = jnp.einsum(
        "sc,sid->cid", owner_weights, returned, preferred_element_type=jnp.float32
    )
    row_range = jnp.arange(shard_rows)
    row_class = jnp.sum((row_range[:, None] >= run_ends[None, :]).astype(jnp.int32), axis=1)
    row_table = (row_class[:, None] == class_range[None, :]).astype(jnp.int32)
    within = row_range - jnp.sum(row_table * starts[None, :], axis=1)
    ffn_rows = jnp.take(
        class_sums.reshape(class_total * capacity, model_width),
        row_class * capacity + within,
        axis=0,
    )
    return (mixed_values + ffn_rows).astype(jnp.bfloat16)


def solution(mesh):
    return jax.shard_map(
        on_device,
        mesh=mesh,
        in_specs=(
            P(("rep", "grp"), "head"),
            P(("rep", "grp"), "head"),
            P(("rep", "grp"), "head"),
            P(("rep", "grp", "head"), None),
            P(),
            P("grp", None, "head"),
            P("grp", None, "head"),
            P("grp", "head", None),
            P(),
            P(("rep", "grp", "head"), None),
            P(("rep", "grp")),
        ),
        out_specs=P(("rep", "grp", "head"), None),
        check_vma=False,
    )
```

profile of v0, /device:TPU:15, one launch (start us, length us, event | category | flops | bytes accessed | tf_op | source)
XLA Modules:
  0.0 142.6 jit_solution(3656424849980349724)
XLA Ops:
  0.0 1.2 copy.33
  1.2 0.9 reshape.175
  2.1 0.8 fusion.23
  2.9 0.2 fusion.15
  3.1 0.3 fusion.36
  3.5 0.4 fusion.16
  3.9 0.2 copy.38
  4.2 0.4 convert_element_type.56
  4.6 4.3 %all_to_all.20 = bf16[2,64,1280]{2,1,0:T(8,128)(2,1)S(1)} all-to-all(bf16[2,64,1280]{2,1,0:T(8,128)(2,1)S(1)} %convert_element_type.56), channel_id=1, replica_groups=mesh['rep'=2,'grp'=8,'head'=2] {'head'}, dimensions={0} | all-to-all | bytes 655360 | tf_op jit(solution)/shard_map/all_to_all | solution.py:72
  9.0 0.2 multiply_reduce_fusion
  9.2 0.2 reduce-window.4
  9.9 1.2 gather_fusion
  11.1 0.2 select_select_fusion
  11.3 0.1 broadcast_in_dim.74
  11.5 50.5 %all_to_all.21 = bf16[16,24,2560]{2,1,0:T(8,128)(2,1)S(1)} all-to-all(bf16[16,24,2560]{2,1,0:T(8,128)(2,1)S(1)} %bitcast.71), channel_id=1, replica_groups=mesh['rep'=2,'grp'=8,'head'=2] {'grp','head'}, dimensions={0} | all-to-all | bytes 3932160 | tf_op jit(solution)/shard_map/all_to_all | solution.py:98
  62.0 8.7 %fusion.5 = f32[384,2048]{1,0:T(8,128)} fusion(bf16[384,2560]{1,0:T(8,128)(2,1)S(1)} %bitcast.73, bf16[1,2560,2048]{2,1,0:T(8,128)(2,1)} %param.16), kind=kOutput, calls=%fused_computation.7 | convolution fusion | flops 4026531840 | bytes 15597568 | tf_op jit(solution)/shard_map/dot_general | solution.py:44
  70.7 17.6 %fusion.7 = bf16[384,2560]{1,0:T(8,128)(2,1)} fusion(bf16[1,2048,2560]{2,1,0:T(8,128)(2,1)} %param.18, f32[384,2048]{1,0:T(8,128)} %fusion.5, bf16[384,2560]{1,0:T(8,128)(2,1)S(1)} %bitcast.74, bf16[1,2560,2048]{2,1,0:T(8,128)(2,1)} %param.17), kind=kOutput, calls=%fused_computation.9 | convolution fusion | flops 8058765312 | bytes 28049408 | tf_op jit(solution)/shard_map/dot_general | solution.py:47
  88.4 5.1 %all-to-all-start.2 = ((bf16[16,24,2560]{2,1,0:T(8,128)(2,1)}), bf16[16,24,2560]{2,1,0:T(8,128)(2,1)}, u32[]{:S(2)}, u32[]{:S(2)}) async-start(bf16[16,24,2560]{2,1,0:T(8,128)(2,1)} %bitcast.19), calls=%async_computation.2 | async-start | bytes 3932160 | tf_op jit(solution)/shard_map/all_to_all | solution.py:55
  93.7 44.5 %all-to-all-done.2 = bf16[16,24,2560]{2,1,0:T(8,128)(2,1)} async-done(((bf16[16,24,2560]{2,1,0:T(8,128)(2,1)}), bf16[16,24,2560]{2,1,0:T(8,128)(2,1)}, u32[]{:S(2)}, u32[]{:S(2)}) %all-to-all-start.2) | async-done | bytes 1966112 | tf_op jit(solution)/shard_map/all_to_all | solution.py:55
  138.2 1.9 %bitcast_reduce_fusion = bf16[8,24,2560]{2,1,0:T(8,128)(2,1)S(1)} fusion(bf16[16,24,2560]{2,1,0:T(8,128)(2,1)} %all-to-all-done.2), kind=kLoop, calls=%fused_computation.11 | loop fusion | flops 491520 | bytes 2949120 | tf_op jit(solution)/shard_map/reduce_sum | solution.py:103
  140.1 0.5 fusion.17
  140.5 0.3 copy.41
  140.9 0.8 gather_fusion.1
  141.7 0.9 add_convert_fusion
  (28 shorter events, 0.8 us)
Async XLA Ops:
  0.0 3.5 %copy-start.1 = (bf16[128,256]{1,0:T(8,128)(2,1)S(1)}, bf16[128,256]{1,0:T(8,128)(2,1)}, u32[]{:S(2)}) copy-start(bf16[128,256]{1,0:T(8,128)(2,1)} %param.13) | copy-start | bytes 196612
  3.5 5.4 %copy-start = (bf16[64,2560]{1,0:T(8,128)(2,1)S(1)}, bf16[64,2560]{1,0:T(8,128)(2,1)}, u32[]{:S(2)}) copy-start(bf16[64,2560]{1,0:T(8,128)(2,1)} %param.14) | copy-start | bytes 983044
  3.9 5.3 %copy-start.2 = (bf16[2560]{0:T(1024)(128)(2,1)S(1)}, bf16[2560]{0:T(1024)(128)(2,1)}, u32[]{:S(2)}) copy-start(bf16[2560]{0:T(1024)(128)(2,1)} %param.15) | copy-start | bytes 15364
  3.9 5.3 %copy-start.4 = (s32[1,4]{1,0:T(1,128)S(1)}, s32[1,4]{1,0:T(1,128)}, u32[]{:S(2)}) copy-start(s32[1,4]{1,0:T(1,128)} %param.20) | copy-start | bytes 52
  3.9 5.5 %copy-start.3 = (s32[8]{0:T(128)S(1)}, s32[8]{0:T(128)}, u32[]{:S(2)}) copy-start(s32[8]{0:T(128)} %param.19) | copy-start | bytes 100
  88.4 49.8 %all-to-all-start.2 = ((bf16[16,24,2560]{2,1,0:T(8,128)(2,1)}), bf16[16,24,2560]{2,1,0:T(8,128)(2,1)}, u32[]{:S(2)}, u32[]{:S(2)}) async-start(bf16[16,24,2560]{2,1,0:T(8,128)(2,1)} %bitcast.19), calls=%async_computation.2 | async-start | bytes 3932160 | tf_op jit(solution)/shard_map/all_to_all | solution.py:55
where the time goes:
time: 143 us
  blocking collectives  54.8 us (38%)
  waiting for transfers between devices  44.5 us (31%)
  matrix products  27.8 us (19%)
  local copies, waits for them, and re-layouts  5.34 us (4%)
  starting transfers between devices  5.09 us (4%)
  other arithmetic  4.78 us (3%)
    all_to_all x1, blocking collectives, on_device(): lax.all_to_all(doubled, ('grp', 'head'), split_axis=0, concat_axis=0, til...  50.5 us
    all_to_all x1, waiting for transfers between devices, answer_back(): lax.all_to_all(partial_out, ('grp', 'head'), split_axis=0, concat_axis=0,...  44.5 us
    dot_general x1, matrix products, class_network(): jnp.dot(hidden, w_down[0], preferred_element_type=jnp.float32)  17.6 us
    dot_general x1, matrix products, class_network(): gate_act = jnp.dot(flattened, w_gate[0], preferred_element_type=jnp.float32)  8.73 us
    all_to_all x1, starting transfers between devices, answer_back(): lax.all_to_all(partial_out, ('grp', 'head'), split_axis=0, concat_axis=0,...  5.09 us
    all_to_all x1, blocking collectives, on_device(): lax.all_to_all(local_heads, 'head', split_axis=0, concat_axis=1, tiled=True)  4.31 us
  transfers between devices with their start and end apart: 1, of which 1 were waited for; matrix products, arithmetic and copies ran while one was open for 0% of the time, Pallas kernels for 0%

commit v1 on v0

--- a/solution.py
+++ b/solution.py
@@ -50,11 +50,6 @@
     return partial_out.reshape(sources, depth_rows, model_width)
 
 
-def answer_back(token_block, w_gate, w_up, w_down):
-    partial_out = class_network(token_block, w_gate, w_up, w_down)
-    return lax.all_to_all(partial_out, ("grp", "head"), split_axis=0, concat_axis=0, tiled=True)
-
-
 def on_device(
     queries,
     key_matrix,
@@ -79,9 +74,11 @@
     group_count = owner_class.shape[0]
     core_total = lax.axis_size("head")
     counts = class_counts[0]
-    run_ends = jnp.cumsum(counts)
+    class_range = jnp.arange(class_total)
+    run_ends = jnp.sum(
+        jnp.where(class_range[None, :] <= class_range[:, None], counts[None, :], 0), axis=1
+    )
     starts = run_ends - counts
-    class_range = jnp.arange(class_total)
     owner_table = (owner_class[:, None] == class_range[None, :]).astype(jnp.int32)
     dest_start = jnp.sum(owner_table * starts[None, :], axis=1)
     dest_count = jnp.sum(owner_table * counts[None, :], axis=1)
@@ -92,18 +89,14 @@
         group_count, capacity, model_width
     )
     outgoing = jnp.where(filled[:, :, None], outgoing, jnp.zeros((), jnp.bfloat16))
-    doubled = jnp.broadcast_to(outgoing[:, None], (group_count, core_total, capacity, model_width))
-    doubled = doubled.reshape(group_count * core_total, capacity, model_width)
-    returned = answer_back(
-        lax.all_to_all(doubled, ("grp", "head"), split_axis=0, concat_axis=0, tiled=True),
-        w_gate,
-        w_up,
-        w_down,
-    )
+    arrived = lax.all_to_all(outgoing, "grp", split_axis=0, concat_axis=0, tiled=True)
+    token_block = lax.all_gather(arrived, "head", axis=0, tiled=True)
+    partial_out = class_network(token_block, w_gate, w_up, w_down)
+    halves = lax.all_to_all(partial_out, "head", split_axis=0, concat_axis=0, tiled=True)
     pair_sum = jnp.sum(
-        returned.reshape(group_count, core_total, capacity, model_width).astype(jnp.float32), axis=1
-    )
-    returned = pair_sum.astype(jnp.bfloat16)
+        halves.reshape(core_total, group_count, capacity, model_width).astype(jnp.float32), axis=0
+    ).astype(jnp.bfloat16)
+    returned = lax.all_to_all(pair_sum, "grp", split_axis=0, concat_axis=0, tiled=True)
     owner_weights = owner_table.astype(jnp.bfloat16)
     class_sums = jnp.einsum(
         "sc,sid->cid", owner_weights, returned, preferred_element_type=jnp.float32

time: 143 us -> 135 us (0.944)
  the two profiles are of different devices: /device:TPU:15 before, /device:TPU:0 now
where the time goes in v1:
time: 135 us
  blocking collectives  42.4 us (31%)
  waiting for transfers between devices  34 us (25%)
  matrix products  29.7 us (22%)
  between operations  13.6 us (10%)
  starting transfers between devices  5.78 us (4%)
  local copies, waits for them, and re-layouts  5.2 us (4%)
  other arithmetic  4.39 us (3%)
    all_to_all x1, blocking collectives, on_device(): lax.all_to_all(outgoing, 'grp', split_axis=0, concat_axis=0, tiled=True)  31.9 us
    all_to_all x1, waiting for transfers between devices, on_device(): lax.all_to_all(pair_sum, 'grp', split_axis=0, concat_axis=0, tiled=True)  24.5 us
    dot_general x1, matrix products, class_network(): jnp.dot(hidden, w_down[0], preferred_element_type=jnp.float32)  17.7 us
    dot_general x1, matrix products, class_network(): gate_act = jnp.dot(flattened, w_gate[0], preferred_element_type=jnp.float32)  10.6 us
    all_gather x1, waiting for transfers between devices, on_device(): token_block = lax.all_gather(arrived, 'head', axis=0, tiled=True)  9.49 us
    all_to_all x1, blocking collectives, on_device(): lax.all_to_all(partial_out, 'head', split_axis=0, concat_axis=0, tiled=True)  6.5 us
    all_to_all x1, starting transfers between devices, on_device(): lax.all_to_all(pair_sum, 'grp', split_axis=0, concat_axis=0, tiled=True)  5.78 us
    all_to_all x1, blocking collectives, on_device(): lax.all_to_all(local_heads, 'head', split_axis=0, concat_axis=1, tiled=True)  4 us
  transfers between devices with their start and end apart: 2, of which 2 were waited for; matrix products, arithmetic and copies ran while one was open for 0% of the time, Pallas kernels for 0%

profile of v1, /device:TPU:0, one launch (start us, length us, event | category | flops | bytes accessed | tf_op | source)
XLA Modules:
  0.0 135.0 jit_solution(9345232837208913943)
XLA Ops:
  6.5 1.2 copy.33
  7.8 0.9 reshape.157
  8.6 0.8 fusion.23
  9.4 0.2 fusion.15
  9.7 0.3 fusion.36
  10.1 0.4 fusion.16
  10.5 0.2 copy.38
  10.7 0.4 convert_element_type.56
  11.1 4.0 %all_to_all.25 = bf16[2,64,1280]{2,1,0:T(8,128)(2,1)S(1)} all-to-all(bf16[2,64,1280]{2,1,0:T(8,128)(2,1)S(1)} %convert_element_type.56), channel_id=1, replica_groups=mesh['rep'=2,'grp'=8,'head'=2] {'head'}, dimensions={0} | all-to-all | bytes 655360 | tf_op jit(solution)/shard_map/all_to_all | solution.py:67
  15.2 0.2 multiply_reduce_fusion
  16.0 1.2 gather_fusion
  17.3 0.2 select_select_fusion
  17.5 31.9 %all_to_all.26 = bf16[8,24,2560]{2,1,0:T(8,128)(2,1)} all-to-all(bf16[8,24,2560]{2,1,0:T(8,128)(2,1)S(1)} %select_select_fusion), channel_id=1, replica_groups=mesh['rep'=2,'grp'=8,'head'=2] {'grp'}, dimensions={0} | all-to-all | bytes 1966080 | tf_op jit(solution)/shard_map/all_to_all | solution.py:92
  49.4 9.5 %all-gather.2.cloned.1.call-done = bf16[16,24,2560]{2,1,0:T(8,128)(2,1)} async-done(((bf16[8,24,2560]{2,1,0:T(8,128)(2,1)}), bf16[16,24,2560]{2,1,0:T(8,128)(2,1)}) %all-gather.2.cloned.1.call-update) | async-done | bytes 1966096 | tf_op jit(solution)/shard_map/all_gather | solution.py:93
  58.9 10.6 %fusion.5 = f32[384,2048]{1,0:T(8,128)} fusion(bf16[384,2560]{1,0:T(8,128)(2,1)} %bitcast.78, bf16[1,2560,2048]{2,1,0:T(8,128)(2,1)} %param.16), kind=kOutput, calls=%fused_computation.7 | convolution fusion | flops 4026531840 | bytes 15597568 | tf_op jit(solution)/shard_map/dot_general | solution.py:44
  69.5 17.7 %fusion.7 = bf16[384,2560]{1,0:T(8,128)(2,1)} fusion(bf16[1,2048,2560]{2,1,0:T(8,128)(2,1)} %param.18, f32[384,2048]{1,0:T(8,128)} %fusion.5, bf16[384,2560]{1,0:T(8,128)(2,1)S(1)} %bitcast.79, bf16[1,2560,2048]{2,1,0:T(8,128)(2,1)} %param.17), kind=kOutput, calls=%fused_computation.9 | convolution fusion | flops 8058765312 | bytes 28049408 | tf_op jit(solution)/shard_map/dot_general | solution.py:47
  87.2 6.5 %all_to_all.27 = bf16[16,24,2560]{2,1,0:T(8,128)(2,1)S(1)} all-to-all(bf16[16,24,2560]{2,1,0:T(8,128)(2,1)} %bitcast.69), channel_id=1, replica_groups=mesh['rep'=2,'grp'=8,'head'=2] {'head'}, dimensions={0} | all-to-all | bytes 3932160 | tf_op jit(solution)/shard_map/all_to_all | solution.py:95
  93.7 1.5 %reduce_sum.87 = bf16[8,24,2560]{2,1,0:T(8,128)(2,1)} reduce(bf16[2,8,24,2560]{3,2,1,0:T(8,128)(2,1)S(1)} %bitcast.67, bf16[]{:T(256)} %constant.53.clone.1), dimensions={0}, to_apply=%region_8.9 | reduce | flops 491520 | bytes 2949122 | tf_op jit(solution)/shard_map/reduce_sum | solution.py:96
  95.2 5.8 %all-to-all-start.3 = ((bf16[8,24,2560]{2,1,0:T(8,128)(2,1)}), bf16[8,24,2560]{2,1,0:T(8,128)(2,1)S(1)}, u32[]{:S(2)}, u32[]{:S(2)}) async-start(bf16[8,24,2560]{2,1,0:T(8,128)(2,1)} %reduce_sum.87), calls=%async_computation.3 | async-start | bytes 1966080 | tf_op jit(solution)/shard_map/all_to_all | solution.py:99
  101.2 24.5 %all-to-all-done.3 = bf16[8,24,2560]{2,1,0:T(8,128)(2,1)S(1)} async-done(((bf16[8,24,2560]{2,1,0:T(8,128)(2,1)}), bf16[8,24,2560]{2,1,0:T(8,128)(2,1)S(1)}, u32[]{:S(2)}, u32[]{:S(2)}) %all-to-all-start.3) | async-done | bytes 983072 | tf_op jit(solution)/shard_map/all_to_all | solution.py:99
  125.7 0.5 fusion.17
  126.1 0.3 copy.41
  126.5 0.8 gather_fusion.1
  127.3 0.9 add_convert_fusion
  (33 shorter events, 1.0 us)
Async XLA Ops:
  6.5 3.5 %copy-start.1 = (bf16[128,256]{1,0:T(8,128)(2,1)S(1)}, bf16[128,256]{1,0:T(8,128)(2,1)}, u32[]{:S(2)}) copy-start(bf16[128,256]{1,0:T(8,128)(2,1)} %param.13) | copy-start | bytes 196612
  6.5 52.4 %all-gather.2.cloned.1.call-start = ((), (), s32[]{:S(2)}) async-start(), calls=%async_computation.4 | async-start | bytes 2949120 | tf_op jit(solution)/shard_map/all_gather | solution.py:93
  10.1 5.1 %copy-start = (bf16[64,2560]{1,0:T(8,128)(2,1)S(1)}, bf16[64,2560]{1,0:T(8,128)(2,1)}, u32[]{:S(2)}) copy-start(bf16[64,2560]{1,0:T(8,128)(2,1)} %param.14) | copy-start | bytes 983044
  10.4 5.0 %copy-start.2 = (bf16[2560]{0:T(1024)(128)(2,1)S(1)}, bf16[2560]{0:T(1024)(128)(2,1)}, u32[]{:S(2)}) copy-start(bf16[2560]{0:T(1024)(128)(2,1)} %param.15) | copy-start | bytes 15364
  10.5 5.0 %copy-start.4 = (s32[1,4]{1,0:T(1,128)S(1)}, s32[1,4]{1,0:T(1,128)}, u32[]{:S(2)}) copy-start(s32[1,4]{1,0:T(1,128)} %param.20) | copy-start | bytes 52
  10.5 5.1 %copy-start.3 = (s32[8]{0:T(128)S(1)}, s32[8]{0:T(128)}, u32[]{:S(2)}) copy-start(s32[8]{0:T(128)} %param.19) | copy-start | bytes 100
  58.9 10.6 %copy-start.5 = (bf16[16,24,2560]{2,1,0:T(8,128)(2,1)S(1)}, bf16[16,24,2560]{2,1,0:T(8,128)(2,1)}, u32[]{:S(2)}) copy-start(bf16[16,24,2560]{2,1,0:T(8,128)(2,1)} %all-gather.2.cloned.1.call-done) | copy-start | bytes 5898244
  95.2 30.4 %all-to-all-start.3 = ((bf16[8,24,2560]{2,1,0:T(8,128)(2,1)}), bf16[8,24,2560]{2,1,0:T(8,128)(2,1)S(1)}, u32[]{:S(2)}, u32[]{:S(2)}) async-start(bf16[8,24,2560]{2,1,0:T(8,128)(2,1)} %reduce_sum.87), calls=%async_computation.3 | async-start | bytes 1966080 | tf_op jit(solution)/shard_map/all_to_all | solution.py:99
Sparse Core Ops, SparseCore 0:
  49.5 9.3 all-gather.1

commit v2 on v1

--- a/solution.py
+++ b/solution.py
@@ -1,8 +1,11 @@
+import functools
 import math
 
 import jax
 import jax.numpy as jnp
 from jax import lax
+from jax.experimental import pallas as pl
+from jax.experimental.pallas import tpu as pltpu
 from jax.sharding import PartitionSpec as P
 
 HEAD_SIZE = 128
@@ -38,16 +41,246 @@
     )
 
 
-def class_network(token_block, w_gate, w_up, w_down):
-    sources, depth_rows, model_width = token_block.shape
-    flattened = token_block.reshape(sources * depth_rows, model_width)
-    gate_act = jnp.dot(flattened, w_gate[0], preferred_element_type=jnp.float32)
-    up_act = jnp.dot(flattened, w_up[0], preferred_element_type=jnp.float32)
-    hidden = (jax.nn.silu(gate_act) * up_act).astype(jnp.bfloat16)
-    partial_out = jnp.dot(hidden, w_down[0], preferred_element_type=jnp.float32).astype(
-        jnp.bfloat16
-    )
-    return partial_out.reshape(sources, depth_rows, model_width)
+def exchange_kernel(
+    group_total,
+    outgoing,
+    gate_hbm,
+    up_hbm,
+    down_hbm,
+    answer,
+    tokens,
+    rows,
+    hidden,
+    part,
+    got,
+    pair,
+    back,
+    gate,
+    up,
+    down,
+    weight_sem,
+    own_sem,
+    out_send,
+    out_recv,
+    near_send,
+    near_recv,
+    part_send,
+    part_recv,
+    back_send,
+    back_recv,
+):
+    me = lax.axis_index("grp")
+    core = lax.axis_index("head")
+    other = 1 - core
+    capacity, width = outgoing.shape[1], outgoing.shape[2]
+    chunks = 2
+    per_chunk = group_total // chunks
+    block = 2 * capacity
+    columns = 256
+
+    def dispatch(k):
+        return pltpu.make_async_remote_copy(
+            src_ref=outgoing.at[k],
+            dst_ref=tokens.at[k, core],
+            send_sem=out_send.at[k],
+            recv_sem=out_recv.at[k],
+            device_id={"grp": lax.rem(me + k, group_total), "head": core},
+            device_id_type=pl.DeviceIdType.MESH,
+        )
+
+    def forward(k):
+        return pltpu.make_async_remote_copy(
+            src_ref=tokens.at[k, core],
+            dst_ref=tokens.at[k, core],
+            send_sem=near_send.at[k],
+            recv_sem=near_recv.at[k],
+            device_id={"head": other},
+            device_id_type=pl.DeviceIdType.MESH,
+        )
+
+    def forwarded(k):
+        return pltpu.make_async_remote_copy(
+            src_ref=tokens.at[k, other],
+            dst_ref=tokens.at[k, other],
+            send_sem=near_send.at[k],
+            recv_sem=near_recv.at[k],
+            device_id={"head": other},
+            device_id_type=pl.DeviceIdType.MESH,
+        )
+
+    def exchange(k):
+        return pltpu.make_async_remote_copy(
+            src_ref=part.at[k, other],
+            dst_ref=got.at[k],
+            send_sem=part_send.at[k],
+            recv_sem=part_recv.at[k],
+            device_id={"head": other},
+            device_id_type=pl.DeviceIdType.MESH,
+        )
+
+    def give_back(k):
+        return pltpu.make_async_remote_copy(
+            src_ref=pair.at[k],
+            dst_ref=back.at[k],
+            send_sem=back_send.at[k],
+            recv_sem=back_recv.at[k],
+            device_id={"grp": lax.rem(me - k + group_total, group_total), "head": core},
+            device_id_type=pl.DeviceIdType.MESH,
+        )
+
+    def each(lower, upper, body):
+        def step(k, carry):
+            body(k)
+            return carry
+
+        lax.fori_loop(lower, upper, step, 0)
+
+    loads = [
+        pltpu.make_async_copy(src.at[0], dst, weight_sem.at[i])
+        for i, (src, dst) in enumerate(((gate_hbm, gate), (up_hbm, up), (down_hbm, down)))
+    ]
+    for load in loads:
+        load.start()
+    own = pltpu.make_async_copy(outgoing.at[0], tokens.at[0, core], own_sem)
+    own.start()
+
+    barrier = pltpu.get_barrier_semaphore()
+
+    def greet(k):
+        pl.semaphore_signal(
+            barrier,
+            inc=1,
+            device_id={"grp": lax.rem(me + k, group_total), "head": core},
+            device_id_type=pl.DeviceIdType.MESH,
+        )
+
+    each(1, group_total, greet)
+    pl.semaphore_signal(
+        barrier, inc=1, device_id={"head": other}, device_id_type=pl.DeviceIdType.MESH
+    )
+    pl.semaphore_wait(barrier, group_total)
+
+    each(1, group_total, lambda k: dispatch(k).start())
+    own.wait()
+    forward(0).start()
+
+    def relay(k):
+        dispatch(k).wait_recv()
+        forward(k).start()
+
+    def network(chunk):
+        first = chunk * per_chunk
+
+        def gather(i):
+            k = first + i
+            forwarded(k).wait_recv()
+            rows[pl.ds(pl.multiple_of(i * block, block), block), :] = (
+                tokens[k].astype(jnp.float32).reshape(block, width).astype(jnp.bfloat16)
+            )
+
+        each(0, per_chunk, gather)
+        if chunk == 0:
+            loads[0].wait()
+            loads[1].wait()
+
+        def widen(j):
+            span = pl.ds(pl.multiple_of(j * columns, columns), columns)
+            gate_act = jnp.dot(rows[...], gate[:, span], preferred_element_type=jnp.float32)
+            up_act = jnp.dot(rows[...], up[:, span], preferred_element_type=jnp.float32)
+            hidden[:, span] = (gate_act / (1.0 + jnp.exp(-gate_act)) * up_act).astype(jnp.bfloat16)
+
+        each(0, hidden.shape[1] // columns, widen)
+        if chunk == 0:
+            loads[2].wait()
+
+        def narrow(j):
+            span = pl.ds(pl.multiple_of(j * columns, columns), columns)
+            total = jnp.dot(hidden[...], down[:, span], preferred_element_type=jnp.float32)
+            part[first : first + per_chunk, :, :, span] = total.reshape(
+                per_chunk, 2, capacity, columns
+            ).astype(jnp.bfloat16)
+
+        each(0, width // columns, narrow)
+        each(first, first + per_chunk, lambda k: exchange(k).start())
+
+    def add_pair(k):
+        exchange(k).wait_recv()
+        pair[k] = (part[k, core].astype(jnp.float32) + got[k].astype(jnp.float32)).astype(
+            jnp.bfloat16
+        )
+
+    def reply(k):
+        add_pair(k)
+        give_back(k).start()
+
+    each(1, per_chunk, relay)
+    network(0)
+    each(per_chunk, group_total, relay)
+    add_pair(0)
+    each(1, per_chunk, reply)
+    network(1)
+    each(per_chunk, group_total, reply)
+
+    answer[0] = pair[0]
+
+    def finish(k):
+        give_back(k).wait_recv()
+        answer[k] = back[k]
+        dispatch(k).wait_send()
+        give_back(k).wait_send()
+
+    each(1, group_total, finish)
+
+    def drain(k):
+        forward(k).wait_send()
+        exchange(k).wait_send()
+
+    each(0, group_total, drain)
+
+
+def exchange_network(outgoing, w_gate, w_up, w_down):
+    group_total, capacity, width = outgoing.shape
+    units = w_gate.shape[2]
+    chunk_rows = group_total * capacity
+    anywhere = pl.BlockSpec(memory_space=pl.ANY)
+    near = pl.BlockSpec(memory_space=pltpu.VMEM)
+    many = pltpu.SemaphoreType.DMA((group_total,))
+    return pl.pallas_call(
+        functools.partial(exchange_kernel, group_total),
+        out_shape=jax.ShapeDtypeStruct(outgoing.shape, jnp.bfloat16),
+        in_specs=[near, anywhere, anywhere, anywhere],
+        out_specs=near,
+        scratch_shapes=[
+            pltpu.VMEM((group_total, 2, capacity, width), jnp.bfloat16),
+            pltpu.VMEM((chunk_rows, width), jnp.bfloat16),
+            pltpu.VMEM((chunk_rows, units), jnp.bfloat16),
+            pltpu.VMEM((group_total, 2, capacity, width), jnp.bfloat16),
+            pltpu.VMEM((group_total, capacity, width), jnp.bfloat16),
+            pltpu.VMEM((group_total, capacity, width), jnp.bfloat16),
+            pltpu.VMEM((group_total, capacity, width), jnp.bfloat16),
+            pltpu.VMEM(w_gate.shape[1:], jnp.bfloat16),
+            pltpu.VMEM(w_up.shape[1:], jnp.bfloat16),
+            pltpu.VMEM(w_down.shape[1:], jnp.bfloat16),
+            pltpu.SemaphoreType.DMA((3,)),
+            pltpu.SemaphoreType.DMA,
+            many,
+            many,
+            many,
+            many,
+            many,
+            many,
+            many,
+            many,
+        ],
+        compiler_params=pltpu.CompilerParams(
+            collective_id=0, has_side_effects=True, vmem_limit_bytes=60 * 1024 * 1024
+        ),
+        cost_estimate=pl.CostEstimate(
+            flops=12 * chunk_rows * width * units,
+            bytes_accessed=6 * width * units,
+            transcendentals=2 * chunk_rows * units,
+        ),
+    )(outgoing, w_gate, w_up, w_down)
 
 
 def on_device(
@@ -72,13 +305,13 @@
     capacity = 3 * shard_rows // 8
     class_total = class_counts.shape[1]
     group_count = owner_class.shape[0]
-    core_total = lax.axis_size("head")
     counts = class_counts[0]
     class_range = jnp.arange(class_total)
     run_ends = jnp.sum(
         jnp.where(class_range[None, :] <= class_range[:, None], counts[None, :], 0), axis=1
     )
     starts = run_ends - counts
+    owner_class = jnp.roll(owner_class, -lax.axis_index("grp"))
     owner_table = (owner_class[:, None] == class_range[None, :]).astype(jnp.int32)
     dest_start = jnp.sum(owner_table * starts[None, :], axis=1)
     dest_count = jnp.sum(owner_table * counts[None, :], axis=1)
@@ -89,14 +322,7 @@
         group_count, capacity, model_width
     )
     outgoing = jnp.where(filled[:, :, None], outgoing, jnp.zeros((), jnp.bfloat16))
-    arrived = lax.all_to_all(outgoing, "grp", split_axis=0, concat_axis=0, tiled=True)
-    token_block = lax.all_gather(arrived, "head", axis=0, tiled=True)
-    partial_out = class_network(token_block, w_gate, w_up, w_down)
-    halves = lax.all_to_all(partial_out, "head", split_axis=0, concat_axis=0, tiled=True)
-    pair_sum = jnp.sum(
-        halves.reshape(core_total, group_count, capacity, model_width).astype(jnp.float32), axis=0
-    ).astype(jnp.bfloat16)
-    returned = lax.all_to_all(pair_sum, "grp", split_axis=0, concat_axis=0, tiled=True)
+    returned = exchange_network(outgoing, w_gate, w_up, w_down)
     owner_weights = owner_table.astype(jnp.bfloat16)
     class_sums = jnp.einsum(
         "sc,sid->cid", owner_weights, returned, preferred_element_type=jnp.float32

time: 135 us -> 83.9 us (0.62)
  Pallas kernels: 0 us -> 63.8 us
  blocking collectives: 42.4 us -> 0 us
  waiting for transfers between devices: 34 us -> 0.01 us
  matrix products: 29.7 us -> 2.62 us
  between operations: 13.6 us -> 0.18 us
  starting transfers between devices: 5.78 us -> 3.46 us
  other arithmetic: 4.39 us -> 6.55 us
  local copies, waits for them, and re-layouts: 5.2 us -> 6.82 us
    pallas_call x0 -> x1, Pallas kernels: none -> 63.8 us  [exchange_network(): pl.pallas_call(functools.partial(exchange_kernel, group_total), out_shape...]
    all_to_all x3 -> x0, blocking collectives: 42.4 us -> none  [the longest x1 31.9 us: on_device(): lax.all_to_all(outgoing, 'grp', split_axis=0, concat_axis=0, tiled=True)]
    dot_general x2 -> x0, matrix products: 28.3 us -> none  [the longest x1 17.7 us: class_network(): jnp.dot(hidden, w_down[0], preferred_element_type=jnp.float32)]
    all_to_all x1, waiting for transfers between devices: 24.5 us -> 0.01 us  [on_device(): lax.all_to_all(local_heads, 'head', split_axis=0, concat_axis=1, tiled=True)]
    all_gather x1 -> x0, waiting for transfers between devices: 9.49 us -> none  [on_device(): token_block = lax.all_gather(arrived, 'head', axis=0, tiled=True)]
    all_to_all x1, starting transfers between devices: 5.78 us -> 3.46 us  [on_device(): lax.all_to_all(local_heads, 'head', split_axis=0, concat_axis=1, tiled=True)]
    reduce_sum x1 -> x0, other arithmetic: 1.54 us -> none  [on_device(): jnp.sum(halves.reshape(core_total, group_count, capacity, model_width).as...]
  transfers between devices with their start and end apart: 2 -> 1, of which waited for: 2 -> 0; matrix products, arithmetic and copies ran while one was open for 0% -> 4% of each run, Pallas kernels for 0% -> 0%
where the time goes in v2:
time: 83.9 us; the launch traced here: 83.4 us
  Pallas kernels  63.8 us (76%)
  local copies, waits for them, and re-layouts  6.82 us (8%)
  other arithmetic  6.55 us (8%)
  starting transfers between devices  3.46 us (4%)
  matrix products  2.62 us (3%)
    pallas_call x1, Pallas kernels, exchange_network(): pl.pallas_call(functools.partial(exchange_kernel, group_total), out_shape...  63.8 us
    all_to_all x1, starting transfers between devices, on_device(): lax.all_to_all(local_heads, 'head', split_axis=0, concat_axis=1, tiled=True)  3.46 us
    dot_general x1, matrix products, on_device(): jnp.einsum('sc,sid->cid', owner_weights, returned, preferred_element_type...  1.68 us
  transfers between devices with their start and end apart: 1, of which 0 were waited for; matrix products, arithmetic and copies ran while one was open for 4% of the time, Pallas kernels for 0%

profile of v2, /device:TPU:0, one launch (start us, length us, event | category | flops | bytes accessed | tf_op | source)
XLA Modules:
  0.0 83.4 jit_solution(15703009438758351158)
XLA Ops:
  0.0 1.2 %copy.26 = bf16[128,1280]{0,1:T(8,128)(2,1)S(1)} copy(bf16[128,1280]{1,0:T(8,128)(2,1)} %param.11) | data formatting | bytes 655360 | tf_op args[0]
  1.2 0.9 %reshape.148 = bf16[128,2,128]{2,1,0:T(2,128)(2,1)S(1)} reshape(bf16[128,256]{1,0:T(8,128)(2,1)} %param.12) | data formatting | bytes 131072 | tf_op jit(solution)/shard_map/reshape | solution.py:19
  2.1 0.8 fusion.10
  2.9 0.2 fusion.4
  3.2 0.3 fusion.22
  3.5 0.9 %reshape.150 = bf16[128,2,128]{2,1,0:T(2,128)(2,1)S(1)} reshape(bf16[128,256]{1,0:T(8,128)(2,1)} %param.13) | data formatting | bytes 131072 | tf_op jit(solution)/shard_map/reshape | solution.py:20
  4.4 0.4 fusion.5
  4.7 0.2 copy.31
  5.0 1.1 %convert_element_type.48 = bf16[2,64,1280]{2,1,0:T(8,128)(2,1)} reshape(bf16[128,2,5,128]{3,2,1,0:T(8,128)(2,1)S(1)} %copy.31) | data formatting | bytes 655360 | tf_op jit(solution)/shard_map/convert_element_type | solution.py:34
  6.1 3.5 %all-to-all-start = ((bf16[2,64,1280]{2,1,0:T(8,128)(2,1)}), bf16[2,64,1280]{2,1,0:T(8,128)(2,1)S(1)}, u32[]{:S(2)}, u32[]{:S(2)}) async-start(bf16[2,64,1280]{2,1,0:T(8,128)(2,1)} %convert_element_type.48), calls=%async_computation | async-start | bytes 655360 | tf_op jit(solution)/shard_map/all_to_all | solution.py:300
  9.6 0.8 select_reduce_fusion.3
  10.3 0.7 fusion.18
  11.1 0.1 select_reduce_fusion.2
  11.2 0.8 pad_add_fusion
  12.1 0.7 select_reduce_fusion.1
  13.1 0.2 multiply_reduce_fusion
  13.4 0.1 multiply_convert_fusion
  13.6 1.2 %gather_fusion = bf16[192,2560]{1,0:T(8,128)(2,1)S(1)} fusion(bf16[64,2560]{1,0:T(8,128)(2,1)S(1)} %multiply_convert_fusion, s32[1024]{0:T(1024)S(1)} %pad_clamp_fusion.1), kind=kCustom, calls=%fused_computation | custom fusion | bytes 1966848 | tf_op jit(solution)/shard_map/jit(_take)/gather | solution.py:321
  14.8 1.2 %select_select_fusion.outgoing = bf16[8,24,2560]{2,1,0:T(8,128)(2,1)} fusion(bf16[8,24,2560]{2,1,0:T(8,128)(2,1)S(1)} %bitcast.47, pred[8,24]{1,0:T(8,128)(4,1)S(1)} %get-tuple-element.8, pred[8,24]{1,0:T(8,128)(4,1)S(1)} %get-tuple-element.7), kind=kLoop, calls=%fused_computation.12 | loop fusion | flops 983040 | bytes 1966464 | tf_op jit(solution)/shard_map/jit(_where)/select_n | solution.py:324
  15.9 63.8 %shard_map.109 = bf16[8,24,2560]{2,1,0:T(8,128)(2,1)} custom-call(bf16[8,24,2560]{2,1,0:T(8,128)(2,1)} %select_select_fusion.outgoing, bf16[1,2560,2048]{2,1,0:T(8,128)(2,1)} %gate_hbm.1, bf16[1,2560,2048]{2,1,0:T(8,128)(2,1)} %up_hbm.1, bf16[1,2048,2560]{2,1,0:T(8,128)(2,1)} %down_hbm.1), custom_call_target="tpu_custom_call" | custom-call | flops 12079595520 | bytes 31457280 | tf_op jit(solution)/shard_map/pallas_call | solution.py:248
  79.7 1.7 %fusion.6 = f32[4,24,2560]{2,0,1:T(4,128)S(1)} fusion(bf16[8,24,2560]{2,1,0:T(8,128)(2,1)} %shard_map.109, s32[8]{0:T(128)S(1)} %dynamic_slice.4), kind=kOutput, calls=%fused_computation.10 | convolution fusion | flops 3932256 | bytes 1966112 | tf_op jit(solution)/shard_map/sc,sid->cid/dot_general | solution.py:327
  81.4 0.3 copy.34
  81.8 0.8 gather_fusion.1
  82.6 0.9 %add_convert_fusion = bf16[64,2560]{1,0:T(8,128)(2,1)} fusion(f32[64,2560]{1,0:T(8,128)S(1)} %gather_fusion.1, pred[64]{0:T(512)(128)(4,1)S(1)} %compare_and_fusion.1, f32[64,2560]{1,0:T(8,128)S(1)} %bitcast.46, bf16[64,2560]{1,0:T(8,128)(2,1)S(1)} %copy-done), kind=kLoop, calls=%fused_computation.14 | loop fusion | flops 819200 | bytes 1966144 | tf_op jit(solution)/shard_map/convert_element_type | solution.py:339
  (19 shorter events, 0.5 us)
Async XLA Ops:
  0.0 13.1 %copy-start = (bf16[64,2560]{1,0:T(8,128)(2,1)S(1)}, bf16[64,2560]{1,0:T(8,128)(2,1)}, u32[]{:S(2)}) copy-start(bf16[64,2560]{1,0:T(8,128)(2,1)} %param.14) | copy-start | bytes 983044
  0.0 13.3 %copy-start.1 = (bf16[2560]{0:T(1024)(128)(2,1)S(1)}, bf16[2560]{0:T(1024)(128)(2,1)}, u32[]{:S(2)}) copy-start(bf16[2560]{0:T(1024)(128)(2,1)} %param.15) | copy-start | bytes 15364
  6.1 6.9 %all-to-all-start = ((bf16[2,64,1280]{2,1,0:T(8,128)(2,1)}), bf16[2,64,1280]{2,1,0:T(8,128)(2,1)S(1)}, u32[]{:S(2)}, u32[]{:S(2)}) async-start(bf16[2,64,1280]{2,1,0:T(8,128)(2,1)} %convert_element_type.48), calls=%async_computation | async-start | bytes 655360 | tf_op jit(solution)/shard_map/all_to_all | solution.py:300

commit v3 on v2

--- a/solution.py
+++ b/solution.py
@@ -11,43 +11,65 @@
 HEAD_SIZE = 128
 
 
-def attend(queries, key_matrix, value_matrix, episode_index):
+def attend(queries, keys, values, episode_column, episode_row, local_heads):
     length = queries.shape[0]
-    kv_count = key_matrix.shape[1] // HEAD_SIZE
-    head_repeats = queries.shape[1] // key_matrix.shape[1]
-    query_tiles = queries.reshape(length, kv_count, head_repeats, HEAD_SIZE)
-    key_tiles = key_matrix.reshape(length, kv_count, HEAD_SIZE)
-    value_tiles = value_matrix.reshape(length, kv_count, HEAD_SIZE)
-    logit_table = jnp.einsum(
-        "envh,ynh->nvey", query_tiles, key_tiles, preferred_element_type=jnp.float32
-    )
-    logit_table = logit_table * (1.0 / math.sqrt(HEAD_SIZE))
-    places = jnp.arange(length)
-    allowed = (episode_index[:, None] == episode_index[None, :]) & (
-        places[None, :] <= places[:, None]
-    )
-    logit_table = jnp.where(allowed, logit_table, -jnp.inf)
-    softmax_probs = jax.nn.softmax(logit_table, axis=-1).astype(jnp.bfloat16)
-    mixed_values = jnp.einsum(
-        "alwn,nam->walm", softmax_probs, value_tiles, preferred_element_type=jnp.float32
-    )
-    return mixed_values.reshape(length, kv_count * head_repeats * HEAD_SIZE).astype(jnp.bfloat16)
-
-
-def normalize(mixed_values, norm_gain):
-    square = jnp.mean(mixed_values * mixed_values, axis=-1, keepdims=True)
-    return (mixed_values * lax.rsqrt(square + 1e-06) * norm_gain.astype(jnp.float32)).astype(
-        jnp.bfloat16
-    )
+    repeats = queries.shape[1] // keys.shape[1]
+    places = lax.broadcasted_iota(jnp.int32, (length, length), 0)
+    sources = lax.broadcasted_iota(jnp.int32, (length, length), 1)
+    allowed = (episode_column[...] == episode_row[...]) & (sources <= places)
+    for j in range(queries.shape[1] // HEAD_SIZE):
+        span = slice(j * HEAD_SIZE, (j + 1) * HEAD_SIZE)
+        shared = slice(j // repeats * HEAD_SIZE, (j // repeats + 1) * HEAD_SIZE)
+        logits = lax.dot_general(
+            queries[:, span],
+            keys[:, shared],
+            (((1,), (1,)), ((), ())),
+            preferred_element_type=jnp.float32,
+        )
+        logits = jnp.where(allowed, logits * (1.0 / math.sqrt(HEAD_SIZE)), -jnp.inf)
+        powers = jnp.exp(logits - jnp.max(logits, axis=1, keepdims=True))
+        probs = (powers / jnp.sum(powers, axis=1, keepdims=True)).astype(jnp.bfloat16)
+        attended = jnp.dot(probs, values[:, shared], preferred_element_type=jnp.float32)
+        local_heads[:, :, span] = attended.astype(jnp.bfloat16).reshape(2, length // 2, HEAD_SIZE)
+
+
+def normalize(residual, mixed, gain, blended, normed):
+    half = mixed.shape[2]
+    width = 2 * half
+    square = 0.0
+    for part in range(2):
+        span = slice(part * half, (part + 1) * half)
+        total = residual[:, span].astype(jnp.float32) + mixed[part].astype(jnp.float32)
+        blended[:, span] = total
+        square += jnp.sum(total * total, axis=1, keepdims=True)
+    scale = lax.rsqrt(square * (1.0 / width) + 1e-06)
+    for part in range(2):
+        span = slice(part * half, (part + 1) * half)
+        normed[:, span] = (
+            blended[:, span] * scale * gain[:, span].astype(jnp.float32)
+        ).astype(jnp.bfloat16)
 
 
 def exchange_kernel(
     group_total,
-    outgoing,
+    queries,
+    keys,
+    values,
+    residual,
+    gain,
+    episode_column,
+    episode_row,
+    pick,
+    merge,
     gate_hbm,
     up_hbm,
     down_hbm,
-    answer,
+    result,
+    local_heads,
+    mixed,
+    blended,
+    normed,
+    outgoing,
     tokens,
     rows,
     hidden,
@@ -68,6 +90,8 @@
     part_recv,
     back_send,
     back_recv,
+    head_send,
+    head_recv,
 ):
     me = lax.axis_index("grp")
     core = lax.axis_index("head")
@@ -141,8 +165,6 @@
     ]
     for load in loads:
         load.start()
-    own = pltpu.make_async_copy(outgoing.at[0], tokens.at[0, core], own_sem)
-    own.start()
 
     barrier = pltpu.get_barrier_semaphore()
 
@@ -158,9 +180,31 @@
     pl.semaphore_signal(
         barrier, inc=1, device_id={"head": other}, device_id_type=pl.DeviceIdType.MESH
     )
+
+    attend(queries, keys, values, episode_column, episode_row, local_heads)
+    mixed[core] = local_heads[core]
     pl.semaphore_wait(barrier, group_total)
-
+    heads = pltpu.make_async_remote_copy(
+        src_ref=local_heads.at[other],
+        dst_ref=mixed.at[core],
+        send_sem=head_send,
+        recv_sem=head_recv,
+        device_id={"head": other},
+        device_id_type=pl.DeviceIdType.MESH,
+    )
+    heads.start()
+    heads.wait()
+    normalize(residual, mixed, gain, blended, normed)
+
+    def choose(j):
+        span = pl.ds(pl.multiple_of(j * columns, columns), columns)
+        chosen = jnp.dot(pick[...], normed[:, span], preferred_element_type=jnp.float32)
+        outgoing[:, :, span] = chosen.reshape(group_total, capacity, columns).astype(jnp.bfloat16)
+
+    each(0, width // columns, choose)
     each(1, group_total, lambda k: dispatch(k).start())
+    own = pltpu.make_async_copy(outgoing.at[0], tokens.at[0, core], own_sem)
+    own.start()
     own.wait()
     forward(0).start()
 
@@ -221,15 +265,24 @@
     network(1)
     each(per_chunk, group_total, reply)
 
-    answer[0] = pair[0]
+    back[0] = pair[0]
 
     def finish(k):
         give_back(k).wait_recv()
-        answer[k] = back[k]
         dispatch(k).wait_send()
         give_back(k).wait_send()
 
     each(1, group_total, finish)
+
+    def combine(j):
+        span = pl.ds(pl.multiple_of(j * columns, columns), columns)
+        replies = back[:, :, span].astype(jnp.float32).reshape(group_total * capacity, columns)
+        sums = jnp.dot(
+            merge[...], replies.astype(jnp.bfloat16), preferred_element_type=jnp.float32
+        )
+        result[:, span] = (blended[:, span] + sums).astype(jnp.bfloat16)
+
+    each(0, width // columns, combine)
 
     def drain(k):
         forward(k).wait_send()
@@ -238,40 +291,39 @@
     each(0, group_total, drain)
 
 
-def exchange_network(outgoing, w_gate, w_up, w_down):
-    group_total, capacity, width = outgoing.shape
-    units = w_gate.shape[2]
+def layer(arrays, weights, group_total, capacity):
+    queries, residual = arrays[0], arrays[3]
+    shard_rows, width = residual.shape
+    length, half = queries.shape
+    units = weights[0].shape[2]
     chunk_rows = group_total * capacity
-    anywhere = pl.BlockSpec(memory_space=pl.ANY)
     near = pl.BlockSpec(memory_space=pltpu.VMEM)
+    blocks = pltpu.VMEM((group_total, capacity, width), jnp.bfloat16)
+    core_blocks = pltpu.VMEM((group_total, 2, capacity, width), jnp.bfloat16)
     many = pltpu.SemaphoreType.DMA((group_total,))
     return pl.pallas_call(
         functools.partial(exchange_kernel, group_total),
-        out_shape=jax.ShapeDtypeStruct(outgoing.shape, jnp.bfloat16),
-        in_specs=[near, anywhere, anywhere, anywhere],
+        out_shape=jax.ShapeDtypeStruct(residual.shape, jnp.bfloat16),
+        in_specs=[near] * len(arrays) + [pl.BlockSpec(memory_space=pl.ANY)] * 3,
         out_specs=near,
         scratch_shapes=[
-            pltpu.VMEM((group_total, 2, capacity, width), jnp.bfloat16),
+            pltpu.VMEM((2, length // 2, half), jnp.bfloat16),
+            pltpu.VMEM((2, length // 2, half), jnp.bfloat16),
+            pltpu.VMEM((shard_rows, width), jnp.float32),
+            pltpu.VMEM((shard_rows, width), jnp.bfloat16),
+            blocks,
+            core_blocks,
             pltpu.VMEM((chunk_rows, width), jnp.bfloat16),
             pltpu.VMEM((chunk_rows, units), jnp.bfloat16),
-            pltpu.VMEM((group_total, 2, capacity, width), jnp.bfloat16),
-            pltpu.VMEM((group_total, capacity, width), jnp.bfloat16),
-            pltpu.VMEM((group_total, capacity, width), jnp.bfloat16),
-            pltpu.VMEM((group_total, capacity, width), jnp.bfloat16),
-            pltpu.VMEM(w_gate.shape[1:], jnp.bfloat16),
-            pltpu.VMEM(w_up.shape[1:], jnp.bfloat16),
-            pltpu.VMEM(w_down.shape[1:], jnp.bfloat16),
-            pltpu.SemaphoreType.DMA((3,)),
-            pltpu.SemaphoreType.DMA,
-            many,
-            many,
-            many,
-            many,
-            many,
-            many,
-            many,
-            many,
-        ],
+            core_blocks,
+            blocks,
+            blocks,
+            blocks,
+        ]
+        + [pltpu.VMEM(w.shape[1:], jnp.bfloat16) for w in weights]
+        + [pltpu.SemaphoreType.DMA((3,)), pltpu.SemaphoreType.DMA]
+        + [many] * 8
+        + [pltpu.SemaphoreType.DMA] * 2,
         compiler_params=pltpu.CompilerParams(
             collective_id=0, has_side_effects=True, vmem_limit_bytes=60 * 1024 * 1024
         ),
@@ -280,7 +332,7 @@
             bytes_accessed=6 * width * units,
             transcendentals=2 * chunk_rows * units,
         ),
-    )(outgoing, w_gate, w_up, w_down)
+    )(*arrays, *weights)
 
 
 def on_device(
@@ -296,47 +348,44 @@
     class_counts,
     episode_index,
 ):
-    local_heads = attend(queries, key_matrix, value_matrix, episode_index)
-    attention_output = lax.all_to_all(local_heads, "head", split_axis=0, concat_axis=1, tiled=True)
-    mixed_values = residual.astype(jnp.float32) + attention_output.astype(jnp.float32)
-    normed = normalize(mixed_values, norm_gain)
     shard_rows = residual.shape[0]
-    model_width = residual.shape[1]
     capacity = 3 * shard_rows // 8
     class_total = class_counts.shape[1]
     group_count = owner_class.shape[0]
     counts = class_counts[0]
     class_range = jnp.arange(class_total)
-    run_ends = jnp.sum(
-        jnp.where(class_range[None, :] <= class_range[:, None], counts[None, :], 0), axis=1
+    starts = jnp.sum(
+        jnp.where(class_range[None, :] < class_range[:, None], counts[None, :], 0), axis=1
     )
-    starts = run_ends - counts
-    owner_class = jnp.roll(owner_class, -lax.axis_index("grp"))
-    owner_table = (owner_class[:, None] == class_range[None, :]).astype(jnp.int32)
-    dest_start = jnp.sum(owner_table * starts[None, :], axis=1)
-    dest_count = jnp.sum(owner_table * counts[None, :], axis=1)
+    group_range = jnp.arange(group_count)
+    dest = (lax.axis_index("grp") + group_range) % group_count
+    owner_table = (owner_class[:, None] == class_range[None, :])[None]
+    owner_table = owner_table & (dest[:, None] == group_range[None, :])[:, :, None]
+    dest_start = jnp.sum(jnp.where(owner_table, starts, 0), axis=(1, 2))
+    dest_count = jnp.sum(jnp.where(owner_table, counts, 0), axis=(1, 2))
     depth_range = jnp.arange(capacity)
-    picked_index = jnp.clip(dest_start[:, None] + depth_range[None, :], 0, shard_rows - 1)
-    filled = depth_range[None, :] < dest_count[:, None]
-    outgoing = jnp.take(normed, picked_index.reshape(-1), axis=0).reshape(
-        group_count, capacity, model_width
+    row_range = jnp.arange(shard_rows)
+    place = jnp.where(
+        depth_range[None, :] < dest_count[:, None], dest_start[:, None] + depth_range[None, :], -1
+    ).reshape(-1)
+    pick = (place[:, None] == row_range[None, :]).astype(jnp.bfloat16)
+    merge = (row_range[:, None] == place[None, :]).astype(jnp.bfloat16)
+    return layer(
+        (
+            queries,
+            key_matrix,
+            value_matrix,
+            residual,
+            norm_gain[None, :],
+            episode_index[:, None],
+            episode_index[None, :],
+            pick,
+            merge,
+        ),
+        (w_gate, w_up, w_down),
+        group_count,
+        capacity,
     )
-    outgoing = jnp.where(filled[:, :, None], outgoing, jnp.zeros((), jnp.bfloat16))
-    returned = exchange_network(outgoing, w_gate, w_up, w_down)
-    owner_weights = owner_table.astype(jnp.bfloat16)
-    class_sums = jnp.einsum(
-        "sc,sid->cid", owner_weights, returned, preferred_element_type=jnp.float32
-    )
-    row_range = jnp.arange(shard_rows)
-    row_class = jnp.sum((row_range[:, None] >= run_ends[None, :]).astype(jnp.int32), axis=1)
-    row_table = (row_class[:, None] == class_range[None, :]).astype(jnp.int32)
-    within = row_range - jnp.sum(row_table * starts[None, :], axis=1)
-    ffn_rows = jnp.take(
-        class_sums.reshape(class_total * capacity, model_width),
-        row_class * capacity + within,
-        axis=0,
-    )
-    return (mixed_values + ffn_rows).astype(jnp.bfloat16)
 
 
 def solution(mesh):

time: 83.9 us -> 77.5 us (0.924)
  Pallas kernels: 63.8 us -> 68.9 us
  starting transfers between devices: 3.46 us -> 0 us
  other arithmetic: 6.55 us -> 3.78 us
  matrix products: 2.62 us -> 0 us
  local copies, waits for them, and re-layouts: 6.82 us -> 4.5 us
    pallas_call x1, Pallas kernels: 63.8 us -> 68.9 us  [layer(): pl.pallas_call(functools.partial(exchange_kernel, group_total), out_shape...]
    all_to_all x1 -> x0, starting transfers between devices: 3.46 us -> none  [on_device(): lax.all_to_all(local_heads, 'head', split_axis=0, concat_axis=1, tiled=True)]
    broadcast_in_dim x0 -> x2, local copies, waits for them, and re-layouts: none -> 2.7 us  [the longest x1 1.39 us: on_device(): episode_index[:, None]]
    dot_general x3 -> x0, matrix products: 2.28 us -> none  [the longest x1 1.68 us: on_device(): jnp.einsum('sc,sid->cid', owner_weights, returned, preferred_element_type...]
    gather x2 -> x0, local copies, waits for them, and re-layouts: 2.01 us -> none  [the longest x1 1.21 us: on_device(): jnp.take(normed, picked_index.reshape(-1), axis=0)]
    reshape x2 -> x0, local copies, waits for them, and re-layouts: 1.73 us -> none  [the longest x1 0.87 us: attend(): key_tiles = key_matrix.reshape(length, kv_count, HEAD_SIZE)]
    convert_element_type x3 -> x0, local copies, waits for them, and re-layouts: 1.38 us -> none  [the longest x2 1.34 us: attend(): mixed_values.reshape(length, kv_count * head_repeats * HEAD_SIZE)]
    select_n x3 -> x2, other arithmetic: 1.17 us -> 0.08 us  [the longest x1 0.07 us: on_device(): jnp.where(depth_range[None, :] < dest_count[:, None], dest_start[:, None]...]
  transfers between devices with their start and end apart: 1 -> 0, of which waited for: 0 -> 0; matrix products, arithmetic and copies ran while one was open for 4% -> 0% of each run, Pallas kernels for 0% -> 0%
where the time goes in v3:
time: 77.5 us; the launch traced here: 77.2 us
  Pallas kernels  68.9 us (89%)
  local copies, waits for them, and re-layouts  4.5 us (6%)
  other arithmetic  3.78 us (5%)
    pallas_call x1, Pallas kernels, layer(): pl.pallas_call(functools.partial(exchange_kernel, group_total), out_shape...  68.9 us
    unnamed x1, local copies, waits for them, and re-layouts  1.72 us

profile of v3, /device:TPU:0, one launch (start us, length us, event | category | flops | bytes accessed | tf_op | source)
XLA Modules:
  0.0 77.2 jit_solution(12983067316873313113)
XLA Ops:
  0.0 0.7 iota_compare_fusion.5
  0.7 0.8 select_reduce_fusion
  1.4 0.1 iota_compare_fusion.2
  1.5 0.9 %fusion.2 = (s32[8]{0:T(128)S(1)}, s32[8]{0:T(128)S(1)}) fusion(s32[4]{0:T(128)} %bitcast.6, pred[8,8]{1,0:T(8,128)(4,1)S(1)} %iota_compare_fusion.2, pred[8,4]{0,1:T(4,128)(4,1)S(1)} %iota_compare_fusion.5, s32[4]{0:T(128)S(1)} %select_reduce_fusion), kind=kLoop, calls=%fused_computation.6 | loop fusion | flops 1264 | bytes 192 | tf_op jit(solution)/shard_map/reduce_sum | solution.py:365
  2.4 0.1 add_select_fusion
  2.5 0.1 select_n.42
  2.5 1.3 %broadcast_in_dim.51.gain = bf16[1,2560]{1,0:T(2,128)(2,1)} reshape(bf16[2560]{0:T(1024)(128)(2,1)} %param.15) | data formatting | bytes 10240 | tf_op jit(solution)/shard_map/broadcast_in_dim | solution.py:379
  3.9 0.6 fusion.1.merge
  4.5 0.7 fusion.pick
  5.2 1.4 %copy.13.episode_column = s32[128,1]{1,0:T(8,128)} copy(s32[128,1]{0,1:T(1,128)} %bitcast.3) | data formatting | bytes 1024 | tf_op jit(solution)/shard_map/broadcast_in_dim | solution.py:380
  6.6 68.9 %shard_map.109 = bf16[64,2560]{1,0:T(8,128)(2,1)} custom-call(bf16[128,1280]{1,0:T(8,128)(2,1)} %queries.1, bf16[128,256]{1,0:T(8,128)(2,1)} %keys.1, bf16[128,256]{1,0:T(8,128)(2,1)} %values.1, bf16[64,2560]{1,0:T(8,128)(2,1)} %residual.1, bf16[1,2560]{1,0:T(2,128)(2,1)} %broadcast_in_dim.51.gain, s32[128,1]{1,0:T(8,128)} %copy.13.episode_column, ...), custom_call_target="tpu_custom_call" | custom-call | flops 12079595520 | bytes 31457280 | tf_op jit(solution)/shard_map/pallas_call | solution.py:304
  75.5 1.7 %copy.15 = bf16[64,2560]{1,0:T(8,128)(2,1)} copy(bf16[64,2560]{1,0:T(8,128)(2,1)} %shard_map.109) | data formatting | bytes 655360
  (1 shorter events, 0.0 us)

commit v4 on v3

--- a/solution.py
+++ b/solution.py
@@ -11,12 +11,13 @@
 HEAD_SIZE = 128
 
 
-def attend(queries, keys, values, episode_column, episode_row, local_heads):
+def attend(queries, keys, values, episode_row, local_heads):
     length = queries.shape[0]
     repeats = queries.shape[1] // keys.shape[1]
     places = lax.broadcasted_iota(jnp.int32, (length, length), 0)
     sources = lax.broadcasted_iota(jnp.int32, (length, length), 1)
-    allowed = (episode_column[...] == episode_row[...]) & (sources <= places)
+    episodes = jnp.broadcast_to(episode_row[...], (length, length))
+    allowed = (episodes.T == episodes) & (sources <= places)
     for j in range(queries.shape[1] // HEAD_SIZE):
         span = slice(j * HEAD_SIZE, (j + 1) * HEAD_SIZE)
         shared = slice(j // repeats * HEAD_SIZE, (j // repeats + 1) * HEAD_SIZE)
@@ -42,11 +43,12 @@
         total = residual[:, span].astype(jnp.float32) + mixed[part].astype(jnp.float32)
         blended[:, span] = total
         square += jnp.sum(total * total, axis=1, keepdims=True)
+    gains = gain[...].astype(jnp.float32)[None, :]
     scale = lax.rsqrt(square * (1.0 / width) + 1e-06)
     for part in range(2):
         span = slice(part * half, (part + 1) * half)
         normed[:, span] = (
-            blended[:, span] * scale * gain[:, span].astype(jnp.float32)
+            blended[:, span] * scale * gains[:, span]
         ).astype(jnp.bfloat16)
 
 
@@ -57,10 +59,9 @@
     values,
     residual,
     gain,
-    episode_column,
     episode_row,
-    pick,
-    merge,
+    owner_class,
+    class_counts,
     gate_hbm,
     up_hbm,
     down_hbm,
@@ -69,6 +70,8 @@
     mixed,
     blended,
     normed,
+    pick,
+    merge,
     outgoing,
     tokens,
     rows,
@@ -97,10 +100,14 @@
     core = lax.axis_index("head")
     other = 1 - core
     capacity, width = outgoing.shape[1], outgoing.shape[2]
-    chunks = 2
-    per_chunk = group_total // chunks
+    half = group_total // 2
+    chunks = ((half, half + half // 2), (half + half // 2, group_total), (0, half))
     block = 2 * capacity
     columns = 256
+
+    def partner(k, sign):
+        side = lax.rem(me // half + k // half, 2)
+        return side * half + lax.rem(lax.rem(me, half) + sign * lax.rem(k, half) + half, half)
 
     def dispatch(k):
         return pltpu.make_async_remote_copy(
@@ -108,7 +115,7 @@
             dst_ref=tokens.at[k, core],
             send_sem=out_send.at[k],
             recv_sem=out_recv.at[k],
-            device_id={"grp": lax.rem(me + k, group_total), "head": core},
+            device_id={"grp": partner(k, 1), "head": core},
             device_id_type=pl.DeviceIdType.MESH,
         )
 
@@ -148,7 +155,7 @@
             dst_ref=back.at[k],
             send_sem=back_send.at[k],
             recv_sem=back_recv.at[k],
-            device_id={"grp": lax.rem(me - k + group_total, group_total), "head": core},
+            device_id={"grp": partner(k, -1), "head": core},
             device_id_type=pl.DeviceIdType.MESH,
         )
 
@@ -172,7 +179,7 @@
         pl.semaphore_signal(
             barrier,
             inc=1,
-            device_id={"grp": lax.rem(me + k, group_total), "head": core},
+            device_id={"grp": partner(k, 1), "head": core},
             device_id_type=pl.DeviceIdType.MESH,
         )
 
@@ -181,7 +188,21 @@
         barrier, inc=1, device_id={"head": other}, device_id_type=pl.DeviceIdType.MESH
     )
 
-    attend(queries, keys, values, episode_column, episode_row, local_heads)
+    depth = lax.broadcasted_iota(jnp.int32, (capacity, residual.shape[0]), 0)
+    place = lax.broadcasted_iota(jnp.int32, (capacity, residual.shape[0]), 1)
+
+    def locate(k):
+        wanted = owner_class[partner(k, 1)]
+        start, count = 0, 0
+        for c in range(class_counts.shape[1]):
+            start += jnp.where(c < wanted, class_counts[0, c], 0)
+            count += jnp.where(c == wanted, class_counts[0, c], 0)
+        hot = (place - start == depth) & (depth < count)
+        pick[pl.ds(pl.multiple_of(k * capacity, 8), capacity), :] = jnp.where(hot, 1.0, 0.0)
+
+    each(0, group_total, locate)
+    merge[...] = pick[...].T.astype(jnp.bfloat16)
+    attend(queries, keys, values, episode_row, local_heads)
     mixed[core] = local_heads[core]
     pl.semaphore_wait(barrier, group_total)
     heads = pltpu.make_async_remote_copy(
@@ -198,22 +219,28 @@
 
     def choose(j):
         span = pl.ds(pl.multiple_of(j * columns, columns), columns)
-        chosen = jnp.dot(pick[...], normed[:, span], preferred_element_type=jnp.float32)
+        chosen = jnp.dot(
+            pick[...].astype(jnp.bfloat16), normed[:, span], preferred_element_type=jnp.float32
+        )
         outgoing[:, :, span] = chosen.reshape(group_total, capacity, columns).astype(jnp.bfloat16)
 
     each(0, width // columns, choose)
-    each(1, group_total, lambda k: dispatch(k).start())
+    each(*chunks[0], lambda k: dispatch(k).start())
     own = pltpu.make_async_copy(outgoing.at[0], tokens.at[0, core], own_sem)
     own.start()
     own.wait()
     forward(0).start()
+    each(*chunks[0], lambda k: dispatch(k).wait_send())
+    each(*chunks[1], lambda k: dispatch(k).start())
+    each(1, half, lambda k: dispatch(k).start())
 
     def relay(k):
         dispatch(k).wait_recv()
         forward(k).start()
 
     def network(chunk):
-        first = chunk * per_chunk
+        first, last = chunks[chunk]
+        held = (last - first) * block
 
         def gather(i):
             k = first + i
@@ -222,16 +249,16 @@
                 tokens[k].astype(jnp.float32).reshape(block, width).astype(jnp.bfloat16)
             )
 
-        each(0, per_chunk, gather)
+        each(0, last - first, gather)
         if chunk == 0:
             loads[0].wait()
             loads[1].wait()
 
         def widen(j):
             span = pl.ds(pl.multiple_of(j * columns, columns), columns)
-            gate_act = jnp.dot(rows[...], gate[:, span], preferred_element_type=jnp.float32)
-            up_act = jnp.dot(rows[...], up[:, span], preferred_element_type=jnp.float32)
-            hidden[:, span] = (gate_act / (1.0 + jnp.exp(-gate_act)) * up_act).astype(jnp.bfloat16)
+            gate_act = jnp.dot(rows[:held], gate[:, span], preferred_element_type=jnp.float32)
+            up_act = jnp.dot(rows[:held], up[:, span], preferred_element_type=jnp.float32)
+            hidden[:held, span] = (gate_act / (1.0 + jnp.exp(-gate_act)) * up_act).astype(jnp.bfloat16)
 
         each(0, hidden.shape[1] // columns, widen)
         if chunk == 0:
@@ -239,13 +266,13 @@
 
         def narrow(j):
             span = pl.ds(pl.multiple_of(j * columns, columns), columns)
-            total = jnp.dot(hidden[...], down[:, span], preferred_element_type=jnp.float32)
-            part[first : first + per_chunk, :, :, span] = total.reshape(
-                per_chunk, 2, capacity, columns
+            total = jnp.dot(hidden[:held], down[:, span], preferred_element_type=jnp.float32)
+            part[first:last, :, :, span] = total.reshape(
+                last - first, 2, capacity, columns
             ).astype(jnp.bfloat16)
 
         each(0, width // columns, narrow)
-        each(first, first + per_chunk, lambda k: exchange(k).start())
+        each(first, last, lambda k: exchange(k).start())
 
     def add_pair(k):
         exchange(k).wait_recv()
@@ -257,22 +284,26 @@
         add_pair(k)
         give_back(k).start()
 
-    each(1, per_chunk, relay)
+    each(*chunks[0], relay)
     network(0)
-    each(per_chunk, group_total, relay)
+    each(*chunks[0], reply)
+    each(*chunks[1], relay)
+    network(1)
+    each(1, half, relay)
+    each(*chunks[1], reply)
+    network(2)
+    each(1, half, reply)
     add_pair(0)
-    each(1, per_chunk, reply)
-    network(1)
-    each(per_chunk, group_total, reply)
 
     back[0] = pair[0]
 
     def finish(k):
         give_back(k).wait_recv()
-        dispatch(k).wait_send()
         give_back(k).wait_send()
 
     each(1, group_total, finish)
+    each(1, half, lambda k: dispatch(k).wait_send())
+    each(*chunks[1], lambda k: dispatch(k).wait_send())
 
     def combine(j):
         span = pl.ds(pl.multiple_of(j * columns, columns), columns)
@@ -304,13 +335,17 @@
     return pl.pallas_call(
         functools.partial(exchange_kernel, group_total),
         out_shape=jax.ShapeDtypeStruct(residual.shape, jnp.bfloat16),
-        in_specs=[near] * len(arrays) + [pl.BlockSpec(memory_space=pl.ANY)] * 3,
+        in_specs=[near] * (len(arrays) - 2)
+        + [pl.BlockSpec(memory_space=pltpu.SMEM)] * 2
+        + [pl.BlockSpec(memory_space=pl.ANY)] * 3,
         out_specs=near,
         scratch_shapes=[
             pltpu.VMEM((2, length // 2, half), jnp.bfloat16),
             pltpu.VMEM((2, length // 2, half), jnp.bfloat16),
             pltpu.VMEM((shard_rows, width), jnp.float32),
             pltpu.VMEM((shard_rows, width), jnp.bfloat16),
+            pltpu.VMEM((chunk_rows, shard_rows), jnp.float32),
+            pltpu.VMEM((shard_rows, chunk_rows), jnp.bfloat16),
             blocks,
             core_blocks,
             pltpu.VMEM((chunk_rows, width), jnp.bfloat16),
@@ -350,37 +385,17 @@
 ):
     shard_rows = residual.shape[0]
     capacity = 3 * shard_rows // 8
-    class_total = class_counts.shape[1]
     group_count = owner_class.shape[0]
-    counts = class_counts[0]
-    class_range = jnp.arange(class_total)
-    starts = jnp.sum(
-        jnp.where(class_range[None, :] < class_range[:, None], counts[None, :], 0), axis=1
-    )
-    group_range = jnp.arange(group_count)
-    dest = (lax.axis_index("grp") + group_range) % group_count
-    owner_table = (owner_class[:, None] == class_range[None, :])[None]
-    owner_table = owner_table & (dest[:, None] == group_range[None, :])[:, :, None]
-    dest_start = jnp.sum(jnp.where(owner_table, starts, 0), axis=(1, 2))
-    dest_count = jnp.sum(jnp.where(owner_table, counts, 0), axis=(1, 2))
-    depth_range = jnp.arange(capacity)
-    row_range = jnp.arange(shard_rows)
-    place = jnp.where(
-        depth_range[None, :] < dest_count[:, None], dest_start[:, None] + depth_range[None, :], -1
-    ).reshape(-1)
-    pick = (place[:, None] == row_range[None, :]).astype(jnp.bfloat16)
-    merge = (row_range[:, None] == place[None, :]).astype(jnp.bfloat16)
     return layer(
         (
             queries,
             key_matrix,
             value_matrix,
             residual,
-            norm_gain[None, :],
-            episode_index[:, None],
+            norm_gain,
             episode_index[None, :],
-            pick,
-            merge,
+            owner_class,
+            class_counts,
         ),
         (w_gate, w_up, w_down),
         group_count,

time: 77.5 us -> 74.5 us (0.961)
  other arithmetic: 3.78 us -> 0 us
  Pallas kernels: 68.9 us -> 72.6 us
  local copies, waits for them, and re-layouts: 4.5 us -> 1.72 us
    pallas_call x1, Pallas kernels: 68.9 us -> 72.6 us  [layer(): pl.pallas_call(functools.partial(exchange_kernel, group_total), out_shape...]
    broadcast_in_dim x2 -> x0, local copies, waits for them, and re-layouts: 2.7 us -> none  [the longest x1 1.39 us: on_device(): episode_index[:, None]]
    reduce_sum x2 -> x0, other arithmetic: 1.64 us -> none  [the longest x1 0.87 us: on_device(): dest_count = jnp.sum(jnp.where(owner_table, counts, 0), axis=(1, 2))]
    convert_element_type x2 -> x0, other arithmetic: 1.32 us -> none  [the longest x1 0.71 us: on_device(): pick = (place[:, None] == row_range[None, :]).astype(jnp.bfloat16)]
where the time goes in v4:
time: 74.5 us; the launch traced here: 74.3 us
  Pallas kernels  72.6 us (97%)
  local copies, waits for them, and re-layouts  1.72 us (2%)
    pallas_call x1, Pallas kernels, layer(): pl.pallas_call(functools.partial(exchange_kernel, group_total), out_shape...  72.6 us
    unnamed x1, local copies, waits for them, and re-layouts  1.72 us

profile of v4, /device:TPU:0, one launch (start us, length us, event | category | flops | bytes accessed | tf_op | source)
XLA Modules:
  0.0 74.3 jit_solution(16303845754772279777)
XLA Ops:
  0.0 72.6 %shard_map.109 = bf16[64,2560]{1,0:T(8,128)(2,1)} custom-call(bf16[128,1280]{1,0:T(8,128)(2,1)} %queries.1, bf16[128,256]{1,0:T(8,128)(2,1)} %keys.1, bf16[128,256]{1,0:T(8,128)(2,1)} %values.1, bf16[64,2560]{1,0:T(8,128)(2,1)} %residual.1, bf16[2560]{0:T(1024)(128)(2,1)} %gain.1, s32[1,128]{1,0:T(1,128)} %bitcast.1, s32[8]{0:T(128)} %owner_class.1, ...), custom_call_target="tpu_custom_call" | custom-call | flops 12079595520 | bytes 31457280 | tf_op jit(solution)/shard_map/pallas_call | solution.py:335
  72.6 1.7 %copy.13 = bf16[64,2560]{1,0:T(8,128)(2,1)} copy(bf16[64,2560]{1,0:T(8,128)(2,1)} %shard_map.109) | data formatting | bytes 655360

commit v5 on v4

--- a/solution.py
+++ b/solution.py
@@ -103,7 +103,8 @@
     half = group_total // 2
     chunks = ((half, half + half // 2), (half + half // 2, group_total), (0, half))
     block = 2 * capacity
-    columns = 256
+    columns = 512
+    narrow_columns = width // 2
 
     def partner(k, sign):
         side = lax.rem(me // half + k // half, 2)
@@ -265,13 +266,13 @@
             loads[2].wait()
 
         def narrow(j):
-            span = pl.ds(pl.multiple_of(j * columns, columns), columns)
+            span = pl.ds(pl.multiple_of(j * narrow_columns, narrow_columns), narrow_columns)
             total = jnp.dot(hidden[:held], down[:, span], preferred_element_type=jnp.float32)
             part[first:last, :, :, span] = total.reshape(
-                last - first, 2, capacity, columns
+                last - first, 2, capacity, narrow_columns
             ).astype(jnp.bfloat16)
 
-        each(0, width // columns, narrow)
+        each(0, width // narrow_columns, narrow)
         each(first, last, lambda k: exchange(k).start())
 
     def add_pair(k):

time: 74.5 us -> 66.4 us (0.89)
  Pallas kernels: 72.6 us -> 64.5 us
    pallas_call x1, Pallas kernels: 72.6 us -> 64.5 us  [layer(): pl.pallas_call(functools.partial(exchange_kernel, group_total), out_shape...]
where the time goes in v5:
time: 66.4 us; the launch traced here: 66.2 us
  Pallas kernels  64.5 us (97%)
  local copies, waits for them, and re-layouts  1.72 us (3%)
    pallas_call x1, Pallas kernels, layer(): pl.pallas_call(functools.partial(exchange_kernel, group_total), out_shape...  64.5 us
    unnamed x1, local copies, waits for them, and re-layouts  1.72 us

profile of v5, /device:TPU:0, one launch (start us, length us, event | category | flops | bytes accessed | tf_op | source)
XLA Modules:
  0.0 66.2 jit_solution(10436030648012177593)
XLA Ops:
  0.0 64.5 %shard_map.109 = bf16[64,2560]{1,0:T(8,128)(2,1)} custom-call(bf16[128,1280]{1,0:T(8,128)(2,1)} %queries.1, bf16[128,256]{1,0:T(8,128)(2,1)} %keys.1, bf16[128,256]{1,0:T(8,128)(2,1)} %values.1, bf16[64,2560]{1,0:T(8,128)(2,1)} %residual.1, bf16[2560]{0:T(1024)(128)(2,1)} %gain.1, s32[1,128]{1,0:T(1,128)} %bitcast.1, s32[8]{0:T(128)} %owner_class.1, ...), custom_call_target="tpu_custom_call" | custom-call | flops 12079595520 | bytes 31457280 | tf_op jit(solution)/shard_map/pallas_call | solution.py:336
  64.5 1.7 %copy.13 = bf16[64,2560]{1,0:T(8,128)(2,1)} copy(bf16[64,2560]{1,0:T(8,128)(2,1)} %shard_map.109) | data formatting | bytes 655360
